TPU v7x, 512 devices: a whole 4x8x8 slice. The times are simulated.
512 devices in a mesh: dp: 64 (over y, z_lo, x), head: 8 (over z_hi, core).
Axes of the slice: x: 4, y: 8, z: 8 (z_hi: 4, z_lo: 2; z = z_hi * 2 + z_lo), core: 2. Of those that a mesh axis runs over, the one named last changes fastest.
Arguments:
- queries: bfloat16 [8192, 16384], P('dp', 'head'), may hold values from -100 to 100
- tree_keys: bfloat16 [8192, 1024], P('dp', 'head'), may hold values from -4 to 4
- tree_values: bfloat16 [8192, 1024], P('dp', 'head'), may hold values from -4 to 4
- cache_keys: bfloat16 [512, 128, 1024], P('dp', None, 'head'), may hold values from -4 to 4
- cache_values: bfloat16 [512, 128, 1024], P('dp', None, 'head'), may hold values from -4 to 4
- parents: int32 [512, 16], P('dp'), may hold values from -1 to 14, as said below
- cache_lengths: int32 [512], P('dp'), may hold values from 16 to 128, as said below
- accepted_counts: int32 [512], P('dp'), may hold values from 4 to 16, as said below
- dest_map: int32 [8192, 1], P('dp'), may hold values from 0 to 63; in each aligned block of 128 rows (0 to 127, 128 to 255, ...) at most 3 rows name the same one
- low_hidden: bfloat16 [8192, 16384], P('dp', 'head'), may hold values from -320 to 320
- mid_hidden: bfloat16 [8192, 16384], P('dp', 'head'), may hold values from -320 to 320
- norm_gains: bfloat16 [3, 16384], P(None, 'head'), may hold values from 0.099609375 to 1.8984375
- merge_down: bfloat16 [16384, 384], P('head'), may hold values from -0.02734375 to 0.02734375
- merge_up: bfloat16 [128, 16384], P(None, 'head'), may hold values from -0.5 to 0.5
- out_grad: bfloat16 [12288, 16384], P('dp', 'head'), may hold values from -0.059814453 to 0.059814453
Outputs:
- gradient_merge_down: float32 [16384, 384], P('head')
- grad_up: float32 [128, 16384], P(None, 'head')
Inputs may be any that keep to these rules, and one draw needn't show every extreme that they name: parents[b, 0] = -1, and 0 <= parents[b, t] < t for t >= 1. `cache_lengths`: some branch has all 128 positions live. A branch accepts its first accepted_counts[b] tree tokens; some branch accepts all 16. `dest_map`: among the rows of one dp index, each trainer shard is named at most 3 times.
All inputs are finite; a program needn't handle non-finite values.
Results may differ from a plain program's by a relative error of at most 0.0055.
Values may be sent and summed in bfloat16 or wider, within the bound.
No kernel may reach another device: no remote copies, remote signals or barrier semaphores. Data moves between devices by JAX's collectives and lax.ppermute only.
A program may use at most 64 MiB of HBM per device.

v0:
```python
import jax
import jax.numpy as jnp
from jax import lax
from jax.sharding import PartitionSpec as P

MODEL_WIDTH = 16384
QHEADS = 128
KVHEADS = 8
HEAD_DIM = 128
TREE = 16
EPSILON = 1e-05
MASKED = -1e30


def ancestors(parents):
    positions = jnp.arange(TREE)
    reached = (parents[:, :, None] == positions[None, None, :]).astype(jnp.float32) + jnp.eye(
        TREE, dtype=jnp.float32
    )[None]
    for repeat_no in range(max(1, (TREE - 1).bit_length())):
        reached = jnp.minimum(
            jnp.einsum("nts,nsu->ntu", reached, reached, precision=lax.Precision.HIGHEST), 1.0
        )
    return reached > 0.5


def verify_attention(
    queries, tree_keys, tree_values, cache_keys, cache_values, parents, cache_lengths
):
    branches = parents.shape[0]
    groups = cache_keys.shape[2] // HEAD_DIM
    group_size = QHEADS // KVHEADS
    cache_len = cache_keys.shape[1]
    score_scale = HEAD_DIM ** (-0.5)
    query_heads = queries.reshape(branches, TREE, groups, group_size, HEAD_DIM)
    far_keys = cache_keys.reshape(branches, cache_len, groups, HEAD_DIM)
    far_values = cache_values.reshape(branches, cache_len, groups, HEAD_DIM)
    near_keys = tree_keys.reshape(branches, TREE, groups, HEAD_DIM)
    near_values = tree_values.reshape(branches, TREE, groups, HEAD_DIM)
    cache_scores = (
        jnp.einsum("btgjd,bpgd->bgjtp", query_heads, far_keys, preferred_element_type=jnp.float32)
        * score_scale
    )
    tree_scores = (
        jnp.einsum("btgjd,bsgd->bgjts", query_heads, near_keys, preferred_element_type=jnp.float32)
        * score_scale
    )
    visible = jnp.arange(cache_len)[None, :] < cache_lengths[:, None]
    cache_scores = jnp.where(visible[:, None, None, None, :], cache_scores, MASKED)
    tree_scores = jnp.where(ancestors(parents)[:, None, None, :, :], tree_scores, MASKED)
    row_max = jnp.maximum(jnp.max(cache_scores, axis=-1), jnp.max(tree_scores, axis=-1))
    cache_weights = jnp.exp(cache_scores - row_max[..., None])
    tree_weights = jnp.exp(tree_scores - row_max[..., None])
    denominator = jnp.sum(cache_weights, axis=-1) + jnp.sum(tree_weights, axis=-1)
    cache_probs = (cache_weights / denominator[..., None]).astype(jnp.bfloat16)
    tree_probs = (tree_weights / denominator[..., None]).astype(jnp.bfloat16)
    attended = jnp.einsum(
        "bgjtp,bpgd->btgjd", cache_probs, far_values, preferred_element_type=jnp.float32
    )
    attended = attended + jnp.einsum(
        "bgjts,bsgd->btgjd", tree_probs, near_values, preferred_element_type=jnp.float32
    )
    return attended.reshape(branches * TREE, groups * group_size * HEAD_DIM).astype(jnp.bfloat16)


def draft_grads(features, grad_in, norm_gains, merge_down, merge_up):
    rank_size = merge_up.shape[0]
    widened = features.astype(jnp.float32)
    squares = jnp.sum(widened * widened, axis=2)
    rescaled_rows = (widened * norm_gains.astype(jnp.float32)[None]).astype(jnp.bfloat16)
    partial_terms = jnp.stack(
        [
            jnp.dot(
                rescaled_rows[:, layer_index],
                merge_down[:, layer_index * rank_size : (layer_index + 1) * rank_size],
                preferred_element_type=jnp.float32,
            )
            for layer_index in range(3)
        ],
        axis=1,
    )
    back_part = lax.dot_general(
        grad_in, merge_up, (((1,), (1,)), ((), ())), preferred_element_type=jnp.float32
    )
    totals, back_rows = lax.psum((squares, back_part), "head")
    inverse = lax.rsqrt(totals / MODEL_WIDTH + EPSILON)
    mixed_rank = lax.psum(jnp.sum(inverse[:, :, None] * partial_terms, axis=1), "head")
    active = jax.nn.silu(mixed_rank).astype(jnp.bfloat16)
    sigmoid_z = jax.nn.sigmoid(mixed_rank)
    grad_mixed = back_rows * sigmoid_z * (1.0 + mixed_rank * (1.0 - sigmoid_z))
    gradient_rescaled = (inverse[:, :, None] * grad_mixed[:, None, :]).astype(jnp.bfloat16)
    gradient_merge_down = jnp.concatenate(
        [
            lax.dot_general(
                rescaled_rows[:, layer_index],
                gradient_rescaled[:, layer_index],
                (((0,), (0,)), ((), ())),
                preferred_element_type=jnp.float32,
            )
            for layer_index in range(3)
        ],
        axis=1,
    )
    grad_up = lax.dot_general(
        active, grad_in, (((0,), (0,)), ((), ())), preferred_element_type=jnp.float32
    )
    return (gradient_merge_down, grad_up)


def body(
    queries,
    tree_keys,
    tree_values,
    cache_keys,
    cache_values,
    parents,
    cache_lengths,
    accepted_counts,
    dest_map,
    low_hidden,
    mid_hidden,
    norm_gains,
    merge_down,
    merge_up,
    out_grad,
):
    row_count = queries.shape[0]
    width = low_hidden.shape[1]
    peer_count = lax.axis_size("dp")
    slot_count = out_grad.shape[0]
    per_peer = slot_count // peer_count
    accepted = jnp.arange(row_count) % TREE < jnp.repeat(
        accepted_counts, TREE, total_repeat_length=row_count
    )
    target = dest_map[:, 0]
    one_hot = (target[:, None] == jnp.arange(peer_count)[None, :]).astype(jnp.float32)
    earlier = (jnp.arange(row_count)[:, None] > jnp.arange(row_count)[None, :]).astype(jnp.float32)
    before = jnp.dot(earlier, one_hot, precision=lax.Precision.HIGHEST)
    slot_rank = jnp.sum(before * one_hot, axis=1).astype(jnp.int32)
    slot_index = target * per_peer + slot_rank
    placer = ((slot_index[None, :] == jnp.arange(slot_count)[:, None]) & accepted[None, :]).astype(
        jnp.bfloat16
    )

    def packed(array):
        return jnp.dot(placer, array, preferred_element_type=jnp.float32).astype(jnp.bfloat16)

    attended = verify_attention(
        queries, tree_keys, tree_values, cache_keys, cache_values, parents, cache_lengths
    )
    all_block = jnp.stack(
        [packed(low_hidden), packed(mid_hidden), packed(attended)], axis=1
    ).reshape(peer_count, per_peer, 3, width)
    features = lax.all_to_all(all_block, "dp", split_axis=0, concat_axis=0, tiled=True).reshape(
        slot_count, 3, width
    )
    gradient_merge_down, grad_up = draft_grads(features, out_grad, norm_gains, merge_down, merge_up)
    summed_down, summed_up = lax.psum((gradient_merge_down, grad_up), "dp")
    return (summed_down, summed_up)


def solution(mesh):
    placed = (
        P("dp", "head"),
        P("dp", "head"),
        P("dp", "head"),
        P("dp", None, "head"),
        P("dp", None, "head"),
        P("dp", None),
        P("dp"),
        P("dp"),
        P("dp", None),
        P("dp", "head"),
        P("dp", "head"),
        P(None, "head"),
        P("head", None),
        P(None, "head"),
        P("dp", "head"),
    )
    return jax.shard_map(
        body,
        mesh=mesh,
        in_specs=placed,
        out_specs=(P("head", None), P(None, "head")),
        check_vma=False,
    )
```

profile of v0, /device:TPU:2, one launch (start us, length us, event | category | flops | bytes accessed | tf_op | source)
XLA Modules:
  0.0 882.6 jit_solution(13178435317797646712)
XLA Ops:
  7.2 0.8 iota_compare_fusion.8
  8.0 1.0 convolution_minimum_fusion.3
  9.1 0.2 convolution_minimum_fusion.2
  9.3 0.2 convolution_minimum_fusion.1
  9.4 0.2 fusion.7
  9.6 1.1 copy.41
  10.8 2.3 fusion.49
  13.1 0.5 fusion.48
  13.8 0.3 fusion.10
  14.1 0.7 fusion.9
  14.8 1.0 fusion.23
  15.8 1.4 fusion.22
  17.4 0.7 fusion.47
  18.2 5.0 fusion.45
  23.2 0.4 convolution_convert_fusion.1
  23.5 0.5 stack.25
  24.1 1.2 convolution_convert_fusion.2
  25.3 2.4 stack.24
  27.8 1.5 copy.31
  29.2 0.3 fusion.50
  29.5 1.4 fusion.6
  31.1 1.2 convolution_convert_fusion
  32.3 3.3 stack.26
  35.6 3.8 pad_maximum_fusion
  39.4 3.2 copy.33
  42.6 12.8 %all-to-all-start = ((bf16[64,3,3,2048]{3,1,2,0:T(4,128)(2,1)}), bf16[64,3,3,2048]{3,1,2,0:T(4,128)(2,1)}, u32[]{:S(2)}, u32[]{:S(2)}) async-start(bf16[64,3,3,2048]{3,1,2,0:T(4,128)(2,1)} %copy.33), calls=%async_computation | async-start | bytes 6291456 | tf_op jit(solution)/shard_map/all_to_all | solution.py:154
  55.4 0.2 all-reduce.7.cloned.1.call-start
  55.7 1.0 fusion.51
  56.7 71.0 %all-to-all-done = bf16[64,3,3,2048]{3,1,2,0:T(4,128)(2,1)} async-done(((bf16[64,3,3,2048]{3,1,2,0:T(4,128)(2,1)}), bf16[64,3,3,2048]{3,1,2,0:T(4,128)(2,1)}, u32[]{:S(2)}, u32[]{:S(2)}) %all-to-all-start) | async-done | bytes 2359328 | tf_op jit(solution)/shard_map/all_to_all | solution.py:154
  127.6 5.6 copy.34
  133.2 8.2 reshape.184
  141.4 3.0 multiply_convert_fusion
  144.4 0.4 convolution_bitcast_fusion
  144.8 0.4 convolution_bitcast_fusion.1
  145.2 0.4 convolution_bitcast_fusion.2
  145.6 3.6 multiply_reduce_fusion
  149.4 18.6 %psum.35 = f32[192,3]{0,1:T(4,128)S(1)} all-reduce(f32[192,3]{0,1:T(4,128)S(1)} %reduce_sum.51), channel_id=1, replica_groups=mesh['dp'=64,'head'=8] {'head'}, use_global_device_ids=true, to_apply=%region_6.7 | all-reduce | flops 576 | bytes 4608 | tf_op jit(solution)/shard_map/psum | solution.py:85
  167.9 0.8 fusion.24
  168.8 75.0 %all-reduce.7.cloned.1.call-done = (f32[192,128]{1,0:T(8,128)}, f32[192,128]{1,0:T(8,128)}) async-done(((f32[192,128]{1,0:T(8,128)}, f32[192,128]{1,0:T(8,128)}), (f32[192,128]{1,0:T(8,128)}, f32[192,128]{1,0:T(8,128)})) %all-reduce.7.cloned.1.call-update) | async-done | bytes 196624 | tf_op jit(solution)/shard_map/psum | solution.py:87
  243.8 2.2 fusion.33
  246.0 1.0 add_multiply_fusion
  247.2 0.3 fusion.13
  247.5 0.3 fusion.12
  247.9 0.3 fusion.11
  248.2 2.0 pad_maximum_fusion.1
  250.3 620.9 %all-reduce.5.cloned.1.call-done = (f32[2048,384]{0,1:T(8,128)}, f32[128,2048]{1,0:T(8,128)}) async-done(((f32[2048,384]{0,1:T(8,128)}, f32[128,2048]{1,0:T(8,128)}), (f32[2048,384]{0,1:T(8,128)}, f32[128,2048]{1,0:T(8,128)})) %all-reduce.5.cloned.1.call-update) | async-done | bytes 4194320 | tf_op jit(solution)/shard_map/psum | solution.py:158
  871.2 3.6 copy.36
  874.8 1.0 copy.53
  (50 shorter events, 0.8 us)
Async XLA Ops:
  7.2 48.5 %copy-start = (bf16[192,2048]{1,0:T(8,128)(2,1)S(1)}, bf16[192,2048]{1,0:T(8,128)(2,1)}, u32[]{:S(2)}) copy-start(bf16[192,2048]{1,0:T(8,128)(2,1)} %param.31) | copy-start | bytes 2359300
  7.2 5.9 copy-start.5
  13.6 3.6 copy-start.17
  13.7 3.8 copy-start.7
  13.7 4.4 copy-start.9
  13.7 4.4 copy-start.10
  13.7 4.4 copy-start.11
  13.7 4.4 copy-start.12
  13.7 4.4 copy-start.13
  13.7 4.4 copy-start.14
  13.7 4.4 copy-start.15
  13.8 9.4 %copy-start.2 = (bf16[128,2048]{1,0:T(8,128)(2,1)S(1)}, bf16[128,2048]{1,0:T(8,128)(2,1)}, u32[]{:S(2)}) copy-start(bf16[128,2048]{1,0:T(8,128)(2,1)} %param.27) | copy-start | bytes 1572868
  14.8 9.3 %copy-start.3 = (bf16[128,2048]{1,0:T(8,128)(2,1)S(1)}, bf16[128,2048]{1,0:T(8,128)(2,1)}, u32[]{:S(2)}) copy-start(bf16[128,2048]{1,0:T(8,128)(2,1)} %param.26) | copy-start | bytes 1572868
  23.5 5.7 copy-start.6
  42.6 13.0 %copy-start.8 = (bf16[3,2048]{1,0:T(4,128)(2,1)S(1)}, bf16[3,2048]{1,0:T(4,128)(2,1)}, u32[]{:S(2)}) copy-start(bf16[3,2048]{1,0:T(4,128)(2,1)} %param.28) | copy-start | bytes 36868
  42.6 13.0 %copy-start.4 = (bf16[128,2048]{1,0:T(8,128)(2,1)S(1)}, bf16[128,2048]{1,0:T(8,128)(2,1)}, u32[]{:S(2)}) copy-start(bf16[128,2048]{1,0:T(8,128)(2,1)} %param.30) | copy-start | bytes 1572868
  42.6 85.0 %all-to-all-start = ((bf16[64,3,3,2048]{3,1,2,0:T(4,128)(2,1)}), bf16[64,3,3,2048]{3,1,2,0:T(4,128)(2,1)}, u32[]{:S(2)}, u32[]{:S(2)}) async-start(bf16[64,3,3,2048]{3,1,2,0:T(4,128)(2,1)} %copy.33), calls=%async_computation | async-start | bytes 6291456 | tf_op jit(solution)/shard_map/all_to_all | solution.py:154
  55.4 188.4 %all-reduce.7.cloned.1.call-start = ((), (), s32[]{:S(2)}) async-start(), calls=%async_computation.2 | async-start | bytes 393216 | tf_op jit(solution)/shard_map/psum | solution.py:87
  141.4 3.1 copy-start.16
  168.7 702.5 %all-reduce.5.cloned.1.call-start = ((), (), s32[]{:S(2)}) async-start(), calls=%async_computation.1 | async-start | bytes 8388608 | tf_op jit(solution)/shard_map/psum | solution.py:158
  871.2 3.6 copy-start.1
Sparse Core Ops, SparseCore 0:
  168.9 74.9 all-reduce.6
  250.4 620.7 all-reduce.4
where the time goes:
time: 884 us; the launch traced here: 883 us
  waiting for transfers between devices  767 us (87%)
  local copies, waits for them, and re-layouts  31.5 us (4%)
  other arithmetic  23.7 us (3%)
  blocking collectives  18.6 us (2%)
  matrix products  14.5 us (2%)
  between operations  14.5 us (2%)
  starting transfers between devices  13 us (1%)
    psum x1, waiting for transfers between devices, body(): summed_down, summed_up = lax.psum((gradient_merge_down, grad_up), 'dp')  621 us
    psum x1, waiting for transfers between devices, draft_grads(): lax.psum(jnp.sum(inverse[:, :, None] * partial_terms, axis=1), 'head')  75 us
    all_to_all x1, waiting for transfers between devices, body(): lax.all_to_all(all_block, 'dp', split_axis=0, concat_axis=0, tiled=True)  71 us
    psum x1, blocking collectives, draft_grads(): totals, back_rows = lax.psum((squares, back_part), 'head')  18.6 us
  transfers between devices with their start and end apart: 3, of which 3 were waited for; matrix products, arithmetic and copies ran while one was open for 0% of the time, Pallas kernels for 0%

commit v1 on v0

--- a/solution.py
+++ b/solution.py
@@ -84,7 +84,9 @@
     )
     totals, back_rows = lax.psum((squares, back_part), "head")
     inverse = lax.rsqrt(totals / MODEL_WIDTH + EPSILON)
-    mixed_rank = lax.psum(jnp.sum(inverse[:, :, None] * partial_terms, axis=1), "head")
+    mixed_rank = jnp.sum(
+        lax.all_gather(jnp.sum(inverse[:, :, None] * partial_terms, axis=1), "head"), axis=0
+    )
     active = jax.nn.silu(mixed_rank).astype(jnp.bfloat16)
     sigmoid_z = jax.nn.sigmoid(mixed_rank)
     grad_mixed = back_rows * sigmoid_z * (1.0 + mixed_rank * (1.0 - sigmoid_z))

time: 884 us -> 825 us (0.933)
  waiting for transfers between devices: 767 us -> 691 us
  blocking collectives: 18.6 us -> 36.6 us
    psum x1, waiting for transfers between devices: 75 us -> 0.01 us  [draft_grads(): totals, back_rows = lax.psum((squares, back_part), 'head')]
    all_gather x0 -> x1, blocking collectives: none -> 18 us  [draft_grads(): lax.all_gather(jnp.sum(inverse[:, :, None] * partial_terms, axis=1), 'head')]
  transfers between devices with their start and end apart: 3 -> 3, of which waited for: 3 -> 2; matrix products, arithmetic and copies ran while one was open for 0% -> 3% of each run, Pallas kernels for 0% -> 0%
where the time goes in v1:
time: 825 us; the launch traced here: 824 us
  waiting for transfers between devices  691 us (84%)
  blocking collectives  36.6 us (4%)
  local copies, waits for them, and re-layouts  31.5 us (4%)
  other arithmetic  24.3 us (3%)
  between operations  14.5 us (2%)
  matrix products  13.6 us (2%)
  starting transfers between devices  13 us (2%)
    psum x1, waiting for transfers between devices, body(): summed_down, summed_up = lax.psum((gradient_merge_down, grad_up), 'dp')  620 us
    all_to_all x1, waiting for transfers between devices, body(): lax.all_to_all(all_block, 'dp', split_axis=0, concat_axis=0, tiled=True)  70.9 us
    psum x1, blocking collectives, draft_grads(): totals, back_rows = lax.psum((squares, back_part), 'head')  18.5 us
    all_gather x1, blocking collectives, draft_grads(): lax.all_gather(jnp.sum(inverse[:, :, None] * partial_terms, axis=1), 'head')  18 us
  transfers between devices with their start and end apart: 3, of which 2 were waited for; matrix products, arithmetic and copies ran while one was open for 3% of the time, Pallas kernels for 0%

profile of v1, /device:TPU:2, one launch (start us, length us, event | category | flops | bytes accessed | tf_op | source)
XLA Modules:
  0.0 824.1 jit_solution(16891515731060342916)
XLA Ops:
  7.2 0.8 iota_compare_fusion.8
  8.0 1.0 convolution_minimum_fusion.3
  9.1 0.2 convolution_minimum_fusion.2
  9.3 0.2 convolution_minimum_fusion.1
  9.4 0.2 fusion.7
  9.6 1.1 copy.48
  10.8 2.3 fusion.49
  13.1 0.5 fusion.48
  13.8 0.3 fusion.10
  14.1 0.7 fusion.9
  14.8 1.0 fusion.23
  15.8 1.4 fusion.22
  17.4 0.7 fusion.47
  18.2 5.1 fusion.45
  23.2 0.4 convolution_convert_fusion.1
  23.6 0.5 stack.25
  24.1 1.2 convolution_convert_fusion.2
  25.4 2.4 stack.24
  27.8 1.5 copy.38
  29.3 0.3 fusion.50
  29.6 1.4 fusion.6
  31.1 1.3 convolution_convert_fusion
  32.4 3.3 stack.26
  35.6 3.8 pad_maximum_fusion
  39.5 3.2 copy.40
  42.7 12.8 %all-to-all-start = ((bf16[64,3,3,2048]{3,1,2,0:T(4,128)(2,1)}), bf16[64,3,3,2048]{3,1,2,0:T(4,128)(2,1)}, u32[]{:S(2)}, u32[]{:S(2)}) async-start(bf16[64,3,3,2048]{3,1,2,0:T(4,128)(2,1)} %copy.40), calls=%async_computation | async-start | bytes 6291456 | tf_op jit(solution)/shard_map/all_to_all | solution.py:156
  55.5 1.0 fusion.51
  56.5 0.2 all-reduce.6.cloned.1.call-start
  56.8 70.9 %all-to-all-done = bf16[64,3,3,2048]{3,1,2,0:T(4,128)(2,1)} async-done(((bf16[64,3,3,2048]{3,1,2,0:T(4,128)(2,1)}), bf16[64,3,3,2048]{3,1,2,0:T(4,128)(2,1)}, u32[]{:S(2)}, u32[]{:S(2)}) %all-to-all-start) | async-done | bytes 2359328 | tf_op jit(solution)/shard_map/all_to_all | solution.py:156
  127.7 5.6 copy.41
  133.3 8.2 reshape.184
  141.5 3.0 multiply_convert_fusion
  144.6 0.4 convolution_bitcast_fusion
  144.9 0.4 convolution_bitcast_fusion.1
  145.3 0.4 convolution_bitcast_fusion.2
  145.7 3.6 multiply_reduce_fusion
  149.5 18.5 %psum.28 = f32[192,3]{0,1:T(4,128)S(1)} all-reduce(f32[192,3]{0,1:T(4,128)S(1)} %reduce_sum.60), channel_id=1, replica_groups=mesh['dp'=64,'head'=8] {'head'}, use_global_device_ids=true, to_apply=%region_6.7 | all-reduce | flops 576 | bytes 4608 | tf_op jit(solution)/shard_map/psum | solution.py:85
  168.2 18.0 %all-gather = f32[1536,128]{1,0:T(8,128)} all-gather(f32[192,128]{1,0:T(8,128)S(1)} %fusion.24), channel_id=2, replica_groups=mesh['dp'=64,'head'=8] {'head'}, dimensions={0}, use_global_device_ids=true | all-gather | bytes 884736 | tf_op jit(solution)/shard_map/all_gather | solution.py:88
  186.2 1.2 reduce_sum.62
  187.4 1.3 fusion.33
  188.7 0.9 add_multiply_fusion
  189.8 0.3 fusion.13
  190.2 0.3 fusion.12
  190.5 0.3 fusion.11
  190.9 2.0 pad_maximum_fusion.1
  192.9 619.7 %all-reduce.6.cloned.1.call-done = (f32[2048,384]{0,1:T(8,128)}, f32[128,2048]{1,0:T(8,128)}) async-done(((f32[2048,384]{0,1:T(8,128)}, f32[128,2048]{1,0:T(8,128)}), (f32[2048,384]{0,1:T(8,128)}, f32[128,2048]{1,0:T(8,128)})) %all-reduce.6.cloned.1.call-update) | async-done | bytes 4194320 | tf_op jit(solution)/shard_map/psum | solution.py:160
  812.6 3.6 copy.43
  816.3 1.0 copy.59
  (52 shorter events, 1.0 us)
Async XLA Ops:
  7.2 48.3 %copy-start = (bf16[192,2048]{1,0:T(8,128)(2,1)S(1)}, bf16[192,2048]{1,0:T(8,128)(2,1)}, u32[]{:S(2)}) copy-start(bf16[192,2048]{1,0:T(8,128)(2,1)} %param.31) | copy-start | bytes 2359300
  7.2 5.9 copy-start.5
  13.6 3.6 copy-start.17
  13.7 3.8 copy-start.7
  13.7 4.4 copy-start.9
  13.7 4.4 copy-start.10
  13.7 4.4 copy-start.11
  13.7 4.4 copy-start.12
  13.7 4.4 copy-start.13
  13.7 4.4 copy-start.14
  13.7 4.4 copy-start.15
  13.8 9.5 %copy-start.2 = (bf16[128,2048]{1,0:T(8,128)(2,1)S(1)}, bf16[128,2048]{1,0:T(8,128)(2,1)}, u32[]{:S(2)}) copy-start(bf16[128,2048]{1,0:T(8,128)(2,1)} %param.27) | copy-start | bytes 1572868
  14.8 9.3 %copy-start.3 = (bf16[128,2048]{1,0:T(8,128)(2,1)S(1)}, bf16[128,2048]{1,0:T(8,128)(2,1)}, u32[]{:S(2)}) copy-start(bf16[128,2048]{1,0:T(8,128)(2,1)} %param.26) | copy-start | bytes 1572868
  23.6 5.7 copy-start.6
  42.7 12.8 %copy-start.4 = (bf16[128,2048]{1,0:T(8,128)(2,1)S(1)}, bf16[128,2048]{1,0:T(8,128)(2,1)}, u32[]{:S(2)}) copy-start(bf16[128,2048]{1,0:T(8,128)(2,1)} %param.30) | copy-start | bytes 1572868
  42.7 14.1 %copy-start.8 = (bf16[3,2048]{1,0:T(4,128)(2,1)S(1)}, bf16[3,2048]{1,0:T(4,128)(2,1)}, u32[]{:S(2)}) copy-start(bf16[3,2048]{1,0:T(4,128)(2,1)} %param.28) | copy-start | bytes 36868
  42.7 85.0 %all-to-all-start = ((bf16[64,3,3,2048]{3,1,2,0:T(4,128)(2,1)}), bf16[64,3,3,2048]{3,1,2,0:T(4,128)(2,1)}, u32[]{:S(2)}, u32[]{:S(2)}) async-start(bf16[64,3,3,2048]{3,1,2,0:T(4,128)(2,1)} %copy.40), calls=%async_computation | async-start | bytes 6291456 | tf_op jit(solution)/shard_map/all_to_all | solution.py:156
  55.5 133.3 %all-reduce.4.cloned.1.call-start = ((), (), s32[]{:S(2)}) async-start(), calls=%async_computation.1 | async-start | bytes 196608 | tf_op jit(solution)/shard_map/psum | solution.py:85
  56.5 756.1 %all-reduce.6.cloned.1.call-start = ((), (), s32[]{:S(2)}) async-start(), calls=%async_computation.2 | async-start | bytes 8388608 | tf_op jit(solution)/shard_map/psum | solution.py:160
  141.5 3.1 copy-start.16
  812.6 3.6 copy-start.1
Sparse Core Ops, SparseCore 0:
  59.2 81.8 all-reduce.3
  193.0 619.5 all-reduce.5
